TPU v7x, 128 devices: a whole 4x4x4 slice. The times are simulated.
128 devices in a mesh: grp: 64 (over z, x, y), mem: 2 (over core).
Axes of the slice: x: 4, y: 4, z: 4, core: 2. Of those that a mesh axis runs over, the one named last changes fastest.
Arguments:
- embeddings: float32 [131072, 1024], P(('grp', 'mem')), may hold values from -6 to 6
- cluster_of: int32 [131072], P(('grp', 'mem')), may hold values from 0 to 383, as said below
Outputs:
- best_similarity: float32 [131072], P(('grp', 'mem'))
Inputs may be any that keep to these rules, and one draw needn't show every extreme that they name: `cluster_of`: cluster c is owned by the device of index (c mod 64) * 2 + (c // 64) mod 2, counted over grp then mem. Among the rows of one device, at most 16 lie in the clusters of one owning device; in every draw the 2 owning devices of one group receive exactly 16 rows from every device. Some clusters have a single row.
All inputs are finite; a program needn't handle non-finite values.
Results may differ from a plain program's by a relative error of at most 0.0014.
Values may be sent and summed in bfloat16 or wider, within the bound.
A program may use at most 64 MiB of HBM per device.

v0:
```python
import math

import jax
import jax.numpy as jnp
from jax import lax
from jax.sharding import PartitionSpec as P


def mask_scores(left_side, right_side):
    left_rows, left_ids, left_anchor = left_side
    right_rows, right_ids, right_anchor = right_side
    scores = jnp.einsum("id,jd->ij", left_rows, right_rows, preferred_element_type=jnp.float32)
    allowed = (
        (left_ids[:, None] == right_ids[None, :])
        & (left_ids[:, None] >= 0)
        & (left_anchor[:, None] != right_anchor[None, :])
    )
    return jnp.where(allowed, scores, -1.0)


def body(embeddings, cluster_of):
    local_rows, feature_count = embeddings.shape
    groups = lax.axis_size("grp")
    members = lax.axis_size("mem")
    owner_count = groups * members
    slot_total = 2 * local_rows
    slot_size = slot_total // owner_count
    factor = lax.rsqrt(
        jnp.mean(embeddings * embeddings, axis=1, keepdims=True) + 1e-06
    ) / math.sqrt(feature_count)
    normed = (embeddings * factor).astype(jnp.bfloat16)
    owner_index = cluster_of % groups * members + cluster_of // groups % members
    onehot = (owner_index[:, None] == jnp.arange(owner_count, dtype=jnp.int32)[None, :]).astype(
        jnp.int32
    )
    before = jnp.cumsum(onehot, axis=0) - onehot
    position = jnp.sum(before * onehot, axis=1)
    slot_index = owner_index * slot_size + position
    device_linear = lax.axis_index("grp") * members + lax.axis_index("mem")
    anchor = device_linear * local_rows + jnp.arange(local_rows, dtype=jnp.int32)
    send_rows = jnp.zeros((slot_total, feature_count), jnp.bfloat16).at[slot_index].set(normed)
    send_ids = jnp.full((slot_total,), -1, jnp.int32).at[slot_index].set(cluster_of)
    send_anchor = jnp.full((slot_total,), -1, jnp.int32).at[slot_index].set(anchor)
    arrived_rows, arrived_ids, arrived_anchor = (
        lax.all_to_all(send_rows, "grp", split_axis=0, concat_axis=0, tiled=True),
        lax.all_to_all(send_ids, "grp", split_axis=0, concat_axis=0, tiled=True),
        lax.all_to_all(send_anchor, "grp", split_axis=0, concat_axis=0, tiled=True),
    )
    arrived = (arrived_rows, arrived_ids, arrived_anchor)
    best_slot = jnp.maximum(
        jnp.full((slot_total,), -1.0, jnp.float32),
        jnp.max(
            mask_scores(
                arrived,
                (
                    lax.all_gather(arrived_rows, "mem", axis=0, tiled=True),
                    lax.all_gather(arrived_ids, "mem", axis=0, tiled=True),
                    lax.all_gather(arrived_anchor, "mem", axis=0, tiled=True),
                ),
            ),
            axis=1,
        ),
    )
    returned = lax.all_to_all(best_slot, "grp", split_axis=0, concat_axis=0, tiled=True)
    return returned[slot_index]


def solution(mesh):
    return jax.shard_map(
        body,
        mesh=mesh,
        in_specs=(P(("grp", "mem"), None), P(("grp", "mem"))),
        out_specs=P(("grp", "mem")),
        check_vma=False,
    )
```

profile of v0, /device:TPU:1, one launch (start us, length us, event | category | flops | bytes accessed | tf_op | source)
XLA Modules:
  0.0 184.2 jit_solution(13327355193318187371)
XLA Ops:
  6.5 0.8 fusion.19
  7.3 0.7 fusion.9
  8.5 2.5 %multiply_reduce_fusion = f32[1024]{0:T(1024)S(1)} fusion(f32[1024,1024]{1,0:T(8,128)} %param.2), kind=kLoop, calls=%fused_computation.6 | loop fusion | flops 2096128 | bytes 4198400 | tf_op jit(solution)/shard_map/reduce_sum | solution.py:29
  11.1 0.4 fusion.4
  11.5 9.2 %scatter_custom_fusion.2 = bf16[2048,1024]{1,0:T(8,128)(2,1)} fusion(s32[1024]{0:T(1024)S(1)} %get-tuple-element.6, f32[1024,1024]{1,0:T(8,128)} %param.2, f32[1024]{0:T(1024)S(1)} %rsqrt_multiply_fusion, bf16[]{:T(256)} %constant.71.clone.1), kind=kCustom, calls=%fused_computation.7 | custom fusion | flops 2097152 | bytes 8392706 | tf_op jit(solution)/shard_map/scatter | solution.py:41
  20.7 62.4 %all_to_all.39 = bf16[64,32,1024]{2,1,0:T(8,128)(2,1)} all-to-all(bf16[64,32,1024]{2,1,0:T(8,128)(2,1)} %bitcast.24), channel_id=1, replica_groups=mesh['grp'=64,'mem'=2] {'grp'}, dimensions={0} | all-to-all | bytes 8388608 | tf_op jit(solution)/shard_map/all_to_all | solution.py:45
  83.1 4.3 %scatter_custom_fusion.1 = s32[2048]{0:T(1024)S(1)} fusion(s32[1024]{0:T(1024)S(1)} %get-tuple-element.6, s32[1024]{0:T(1024)S(1)} %get-tuple-element.7, s32[]{:T(128)} %constant.59.clone.1), kind=kCustom, calls=%fused_computation.37 | custom fusion | bytes 8196 | tf_op jit(solution)/shard_map/scatter | solution.py:43
  87.4 0.7 all_to_all.28
  88.1 6.1 %all-to-all-start.1 = ((s32[64,32,1]{1,2,0:T(1,128)}), s32[64,32,1]{1,2,0:T(1,128)S(1)}, u32[]{:S(2)}, u32[]{:S(2)}) async-start(s32[64,32,1]{1,2,0:T(1,128)} %bitcast.5), calls=%async_computation.1 | async-start | bytes 65536 | tf_op jit(solution)/shard_map/all_to_all | solution.py:47
  94.2 4.3 %scatter_custom_fusion = s32[2048]{0:T(1024)S(1)} fusion(s32[1024]{0:T(1024)S(1)} %get-tuple-element.6, s32[1024]{0:T(1024)S(1)} %copy-done, s32[]{:T(128)} %constant.59.clone.1), kind=kCustom, calls=%fused_computation.39 | custom fusion | bytes 8196 | tf_op jit(solution)/shard_map/scatter | solution.py:42
  98.6 0.7 all_to_all.26
  99.2 3.4 %all-to-all-done.1 = s32[64,32,1]{1,2,0:T(1,128)S(1)} async-done(((s32[64,32,1]{1,2,0:T(1,128)}), s32[64,32,1]{1,2,0:T(1,128)S(1)}, u32[]{:S(2)}, u32[]{:S(2)}) %all-to-all-start.1) | async-done | bytes 8224 | tf_op jit(solution)/shard_map/all_to_all | solution.py:47
  102.6 6.4 %all-to-all-start = ((s32[64,32,1]{1,2,0:T(1,128)}), s32[64,32,1]{1,2,0:T(1,128)S(1)}, u32[]{:S(2)}, u32[]{:S(2)}) async-start(s32[64,32,1]{1,2,0:T(1,128)} %bitcast.4), calls=%async_computation | async-start | bytes 65536 | tf_op jit(solution)/shard_map/all_to_all | solution.py:46
  109.0 0.5 broadcast.96
  109.5 0.7 reduce.9
  110.3 7.1 %all-to-all-done = s32[64,32,1]{1,2,0:T(1,128)S(1)} async-done(((s32[64,32,1]{1,2,0:T(1,128)}), s32[64,32,1]{1,2,0:T(1,128)S(1)}, u32[]{:S(2)}, u32[]{:S(2)}) %all-to-all-start) | async-done | bytes 8224 | tf_op jit(solution)/shard_map/all_to_all | solution.py:46
  117.4 0.7 reduce.10
  118.2 6.0 %all_gather.10 = s32[4096]{0:T(1024)S(1)} all-gather(s32[2048]{0:T(1024)S(1)} %ne.44), channel_id=1, replica_groups=mesh['grp'=64,'mem'=2] {'mem'}, dimensions={0}, use_global_device_ids=true | all-gather | bytes 24576 | tf_op jit(solution)/shard_map/all_gather | solution.py:58
  124.2 2.0 %all_gather.9 = s32[4096]{0:T(1024)S(1)} all-gather(s32[2048]{0:T(1024)S(1)} %eq.48), channel_id=1, replica_groups=mesh['grp'=64,'mem'=2] {'mem'}, dimensions={0}, use_global_device_ids=true | all-gather | bytes 24576 | tf_op jit(solution)/shard_map/all_gather | solution.py:57
  126.2 26.4 %select_reduce_fusion = f32[2048]{0:T(1024)S(1)} fusion(bf16[2048,1024]{1,0:T(8,128)(2,1)} %bitcast.23, bf16[4096,1024]{1,0:T(8,128)(2,1)} %all-gather.2.cloned.1.call-done, s32[4096]{0:T(1024)S(1)} %all_gather.10, s32[4096]{0:T(1024)S(1)} %all_gather.9, s32[2048]{0:T(1024)S(1)} %ne.44, s32[2048]{0:T(1024)S(1)} %eq.48, ...), kind=kOutput, calls=%fused_computation.4 | convolution fusion | flops 17230198784 | bytes 12642304 | tf_op jit(solution)/shard_map/id,jd->ij/dot_general | solution.py:12
  152.6 12.9 %all_to_all.40 = f32[64,32,1]{1,2,0:T(1,128)S(1)} all-to-all(f32[64,32,1]{1,2,0:T(1,128)S(1)} %bitcast.25), channel_id=1, replica_groups=mesh['grp'=64,'mem'=2] {'grp'}, dimensions={0} | all-to-all | bytes 16384 | tf_op jit(solution)/shard_map/all_to_all | solution.py:64
  165.5 0.5 broadcast.98
  166.0 0.7 reduce.11
  166.8 10.5 %gather_fusion = f32[1024]{0:T(1024)} fusion(f32[2048]{0:T(1024)S(1)} %all_to_all.34, s32[1024]{0:T(1024)S(1)} %get-tuple-element.5), kind=kCustom, calls=%fused_computation | custom fusion | bytes 12288 | tf_op jit(solution)/shard_map/gather | solution.py:65
  (20 shorter events, 0.8 us)
Async XLA Ops:
  6.5 4.9 %copy-start = (s32[1024]{0:T(1024)S(1)}, s32[1024]{0:T(1024)}, u32[]{:S(2)}) copy-start(s32[1024]{0:T(1024)} %param.3) | copy-start | bytes 12292
  6.5 119.6 %all-gather.2.cloned.1.call-start = ((), (), s32[]{:S(2)}) async-start(), calls=%async_computation.4 | async-start | bytes 12582912 | tf_op jit(solution)/shard_map/all_gather | solution.py:56
  88.1 14.5 %all-to-all-start.1 = ((s32[64,32,1]{1,2,0:T(1,128)}), s32[64,32,1]{1,2,0:T(1,128)S(1)}, u32[]{:S(2)}, u32[]{:S(2)}) async-start(s32[64,32,1]{1,2,0:T(1,128)} %bitcast.5), calls=%async_computation.1 | async-start | bytes 65536 | tf_op jit(solution)/shard_map/all_to_all | solution.py:47
  102.6 14.8 %all-to-all-start = ((s32[64,32,1]{1,2,0:T(1,128)}), s32[64,32,1]{1,2,0:T(1,128)S(1)}, u32[]{:S(2)}, u32[]{:S(2)}) async-start(s32[64,32,1]{1,2,0:T(1,128)} %bitcast.4), calls=%async_computation | async-start | bytes 65536 | tf_op jit(solution)/shard_map/all_to_all | solution.py:46
Sparse Core Ops, SparseCore 0:
  83.2 22.1 all-gather.1
where the time goes:
time: 185 us; the launch traced here: 184 us
  blocking collectives  83.2 us (45%)
  matrix products  26.4 us (14%)
  local copies, waits for them, and re-layouts  22 us (12%)
  other arithmetic  16.1 us (9%)
  between operations  13.5 us (7%)
  starting transfers between devices  12.5 us (7%)
  waiting for transfers between devices  10.5 us (6%)
    all_to_all x1, blocking collectives, body(): lax.all_to_all(send_rows, 'grp', split_axis=0, concat_axis=0, tiled=True)  62.4 us
    dot_general x1, matrix products, mask_scores(): jnp.einsum('id,jd->ij', left_rows, right_rows, preferred_element_type=jnp...  26.4 us
    all_to_all x1, blocking collectives, body(): lax.all_to_all(best_slot, 'grp', split_axis=0, concat_axis=0, tiled=True)  12.9 us
    gather x1, local copies, waits for them, and re-layouts, body(): return returned[slot_index]  10.5 us
    scatter x1, other arithmetic, body(): jnp.zeros((slot_total, feature_count), jnp.bfloat16).at[slot_index]  9.22 us
    all_to_all x1, waiting for transfers between devices, body(): lax.all_to_all(send_ids, 'grp', split_axis=0, concat_axis=0, tiled=True)  7.08 us
    all_to_all x1, starting transfers between devices, body(): lax.all_to_all(send_ids, 'grp', split_axis=0, concat_axis=0, tiled=True)  6.38 us
    all_to_all x1, starting transfers between devices, body(): lax.all_to_all(send_anchor, 'grp', split_axis=0, concat_axis=0, tiled=True)  6.12 us
  transfers between devices with their start and end apart: 3, of which 2 were waited for; matrix products, arithmetic and copies ran while one was open for 6% of the time, Pallas kernels for 0%

commit v1 on v0

v1 whole, which is shorter than its diff:
```python
import functools
import math

import jax
import jax.numpy as jnp
from jax import lax
from jax.experimental import pallas as pl
from jax.experimental.pallas import tpu as pltpu
from jax.sharding import PartitionSpec as P

MESH = pl.DeviceIdType.MESH
STEP = 115
BACK = 59
DEVS = 128
SLOT = 16
GROUP = 16
CHUNK = GROUP * SLOT
CHUNKS = DEVS // GROUP
NT = (((1,), (1,)), ((), ()))


def dot(a, b, dims=(((1,), (0,)), ((), ()))):
    return lax.dot_general(a, b, dims, preferred_element_type=jnp.float32)


def iota(shape, dim):
    return lax.broadcasted_iota(jnp.int32, shape, dim)


def kernel(
    emb, ids, out,
    raw, normed, send, recv, tag_out, tag_in, best_out, best_in,
    tag_col, tag_row, row_max, col_max,
    load_sem, send_sem, recv_sem, tag_sems, best_sems,
):
    rows, width = raw.shape
    grp, core = lax.axis_index("grp"), lax.axis_index("mem")
    z, x, y = grp // 16, (grp // 4) % 4, grp % 4

    def shift(k):
        q = (k * STEP) % DEVS
        return q // 32, (q // 8) % 4, (q // 2) % 4, q % 2

    def to(k):
        dz, dx, dy, dc = shift(k)
        way = 1 - 2 * core
        g = ((z + way * dz + 4) % 4) * 16 + ((x + way * dx + 4) % 4) * 4 + (y + way * dy + 4) % 4
        return g, (core + dc) % 2

    def origin(k):
        dz, dx, dy, dc = shift(k)
        there = (core + dc) % 2
        way = 1 - 2 * there
        g = ((z - way * dz + 4) % 4) * 16 + ((x - way * dx + 4) % 4) * 4 + (y - way * dy + 4) % 4
        return g, there

    part = rows // 8
    loads = [
        pltpu.make_async_copy(
            emb.at[pl.ds(i * part, part)], raw.at[pl.ds(i * part, part)], load_sem.at[i]
        )
        for i in range(8)
    ]
    for load in loads:
        load.start()

    barrier = pltpu.get_barrier_semaphore()

    def greet(k, c):
        pl.semaphore_signal(barrier, inc=1, device_id=to(k), device_id_type=MESH)
        return c

    lax.fori_loop(1, DEVS, greet, 0)

    cluster = ids[...]
    o_grp, o_mem, layer = cluster & 63, (cluster >> 6) & 1, cluster >> 7
    way = 1 - 2 * core
    dz = (way * ((o_grp >> 4) - z)) & 3
    dx = (way * (((o_grp >> 2) & 3) - x)) & 3
    dy = (way * ((o_grp & 3) - y)) & 3
    dc = (o_mem - core) & 1
    place = ((dz * 32 + dx * 8 + dy * 2 + dc) * BACK) & (DEVS - 1)
    owner_is = (iota((DEVS, rows), 0) == place).astype(jnp.float32)
    owner_bf = owner_is.astype(jnp.bfloat16)
    upper = (iota((256, 256), 0) < iota((256, 256), 1)).astype(jnp.bfloat16)
    before = jnp.zeros((DEVS, 1), jnp.float32)
    ranks = []
    for i in range(rows // 256):
        block = owner_is[:, i * 256 : (i + 1) * 256]
        ahead = dot(owner_bf[:, i * 256 : (i + 1) * 256], upper) + before
        ranks.append(jnp.sum(block * ahead, axis=0, keepdims=True))
        before = before + jnp.sum(block, axis=1, keepdims=True)
    rank = jnp.concatenate(ranks, axis=1).astype(jnp.int32)
    slot = place * SLOT + rank
    rank_is = iota((DEVS, rows), 0) == rank
    tags = dot(
        owner_bf, jnp.where(rank_is, (layer + 1).astype(jnp.float32), 0.0).astype(jnp.bfloat16), NT
    )
    tag_out[...] = tags.reshape(DEVS, 1, DEVS)
    tag_in[0] = tag_out[0]

    for i in range(8):
        loads[i].wait()
        block = raw[i * part : (i + 1) * part, :]
        factor = lax.rsqrt(jnp.mean(block * block, axis=1, keepdims=True) + 1e-06) / math.sqrt(width)
        normed[i * part : (i + 1) * part, :] = (block * factor).astype(jnp.bfloat16)

    def row_copy(k, t):
        at = pl.ds(pl.multiple_of(k * SLOT, SLOT), SLOT)
        return pltpu.make_async_remote_copy(
            src_ref=send.at[at], dst_ref=recv.at[at], send_sem=send_sem, recv_sem=recv_sem.at[t],
            device_id=to(k), device_id_type=MESH,
        )

    def tag_copy(k):
        return pltpu.make_async_remote_copy(
            src_ref=tag_out.at[k], dst_ref=tag_in.at[k], send_sem=tag_sems.at[0], recv_sem=tag_sems.at[1],
            device_id=to(k), device_id_type=MESH,
        )

    def best_copy(k):
        return pltpu.make_async_remote_copy(
            src_ref=best_out.at[k], dst_ref=best_in.at[k], send_sem=best_sems.at[0], recv_sem=best_sems.at[1],
            device_id=origin(k), device_id_type=MESH,
        )

    def whole(src, dst, sems, lo, n):
        return pltpu.make_async_remote_copy(
            src_ref=src.at[pl.ds(lo, n)], dst_ref=dst.at[pl.ds(lo, n)], send_sem=sems[0], recv_sem=sems[1],
            device_id=to(1), device_id_type=MESH,
        )

    for t in range(CHUNKS):
        pick = (iota((CHUNK, rows), 0) + t * CHUNK == slot).astype(jnp.float32).astype(jnp.bfloat16)
        send[t * CHUNK : (t + 1) * CHUNK, :] = dot(pick, normed[...]).astype(jnp.bfloat16)
        if t == 0:
            recv[:SLOT, :] = send[:SLOT, :]
            pl.semaphore_wait(barrier, DEVS - 1)

        def start(k, c):
            row_copy(k, t).start()
            return c

        lax.fori_loop(max(1, t * GROUP), (t + 1) * GROUP, start, 0)
        if t == 0:

            def start_tag(k, c):
                tag_copy(k).start()
                return c

            lax.fori_loop(1, DEVS, start_tag, 0)

    whole(tag_out, tag_in, (tag_sems.at[0], tag_sems.at[1]), 1, DEVS - 1).wait()
    own_lane = iota((CHUNK, DEVS), 1) == iota((CHUNK, DEVS), 0) % SLOT
    for t in range(CHUNKS):
        spread = jnp.broadcast_to(tag_in[t * GROUP : (t + 1) * GROUP], (GROUP, SLOT, DEVS))
        tag = jnp.where(own_lane, spread.reshape(CHUNK, DEVS), 0.0).astype(jnp.bfloat16)
        tag_col[t * CHUNK : (t + 1) * CHUNK, :] = dot(tag, jnp.ones((DEVS, DEVS), jnp.bfloat16))
        along = dot(jnp.ones((8, DEVS), jnp.bfloat16), tag, NT)
        tag_row[:, t * CHUNK : (t + 1) * CHUNK] = jnp.where(along == 0.0, -1.0, along)
    col_max[...] = jnp.full(col_max.shape, -1.0, jnp.float32)

    def tile(t, j, diagonal, best):
        at_t = pl.ds(pl.multiple_of(t * CHUNK, CHUNK), CHUNK)
        at_j = pl.ds(pl.multiple_of(j * CHUNK, CHUNK), CHUNK)
        scores = dot(recv[at_t, :], recv[at_j, :], NT)
        col_tag = tag_col[at_t, :]
        row_tag = tag_row[0:1, at_j]
        allowed = jnp.concatenate([col_tag, col_tag], axis=1) == row_tag
        if diagonal:
            allowed = allowed & (iota((CHUNK, CHUNK), 0) != iota((CHUNK, CHUNK), 1))
        scores = jnp.where(allowed, scores, -1.0)
        if not diagonal:
            col_max[:, at_j] = jnp.maximum(
                col_max[:, at_j], jnp.max(scores.reshape(CHUNK // 8, 8, CHUNK), axis=0)
            )
        return jnp.maximum(best, jnp.maximum(scores[:, :128], scores[:, 128:]))

    for t in range(CHUNKS):
        lo = 1 if t == 0 else t * GROUP
        n = (t + 1) * GROUP - lo
        whole(send, recv, (send_sem, recv_sem.at[t]), lo * SLOT, n * SLOT).wait_recv()
        best = tile(t, t, True, jnp.full((CHUNK, 128), -1.0, jnp.float32))
        if t:
            best = lax.fori_loop(0, t, lambda j, b: tile(t, j, False, b), best)
        row_max[t * CHUNK : (t + 1) * CHUNK, :] = best

    eye = iota((128, 128), 0) == iota((128, 128), 1)
    for t in range(CHUNKS):
        along = jnp.max(col_max[:, t * CHUNK : (t + 1) * CHUNK], axis=0, keepdims=True)
        turned = jnp.concatenate(
            [jnp.where(eye, along[:, :128], -1.0), jnp.where(eye, along[:, 128:], -1.0)], axis=0
        )
        best = jnp.max(jnp.maximum(row_max[t * CHUNK : (t + 1) * CHUNK, :], turned), axis=1, keepdims=True)
        laid = jnp.where(own_lane, best, -1.0).reshape(GROUP, SLOT, DEVS)
        best_out[t * GROUP : (t + 1) * GROUP] = jnp.max(laid, axis=1, keepdims=True)

        def give(k, c):
            best_copy(k).start()
            return c

        lax.fori_loop(max(1, t * GROUP), (t + 1) * GROUP, give, 0)
        if t == 0:
            best_in[0] = best_out[0]

    whole(send, recv, (send_sem, recv_sem.at[0]), SLOT, (DEVS - 1) * SLOT).wait_send()
    whole(best_out, best_in, (best_sems.at[0], best_sems.at[1]), 1, DEVS - 1).wait()
    rank_bf = rank_is.astype(jnp.float32).astype(jnp.bfloat16)
    rest = best_in[...].reshape(DEVS, DEVS)
    found = jnp.zeros((DEVS, rows), jnp.float32)
    for _ in range(3):
        piece = rest.astype(jnp.bfloat16)
        rest = rest - piece.astype(jnp.float32)
        found = found + dot(piece, rank_bf)
    out[...] = jnp.sum(owner_is * found, axis=0, keepdims=True)


def body(embeddings, cluster_of):
    rows, width = embeddings.shape
    slots = DEVS * SLOT
    best = pl.pallas_call(
        kernel,
        out_shape=jax.ShapeDtypeStruct((1, rows), jnp.float32),
        in_specs=[pl.BlockSpec(memory_space=pl.ANY), pl.BlockSpec(memory_space=pltpu.VMEM)],
        out_specs=pl.BlockSpec(memory_space=pltpu.VMEM),
        scratch_shapes=[
            pltpu.VMEM((rows, width), jnp.float32),
            pltpu.VMEM((rows, width), jnp.bfloat16),
            pltpu.VMEM((slots, width), jnp.bfloat16),
            pltpu.VMEM((slots, width), jnp.bfloat16),
            pltpu.VMEM((DEVS, 1, DEVS), jnp.float32),
            pltpu.VMEM((DEVS, 1, DEVS), jnp.float32),
            pltpu.VMEM((DEVS, 1, DEVS), jnp.float32),
            pltpu.VMEM((DEVS, 1, DEVS), jnp.float32),
            pltpu.VMEM((slots, 128), jnp.float32),
            pltpu.VMEM((8, slots), jnp.float32),
            pltpu.VMEM((slots, 128), jnp.float32),
            pltpu.VMEM((8, slots), jnp.float32),
            pltpu.SemaphoreType.DMA((8,)),
            pltpu.SemaphoreType.DMA,
            pltpu.SemaphoreType.DMA((CHUNKS,)),
            pltpu.SemaphoreType.DMA((2,)),
            pltpu.SemaphoreType.DMA((2,)),
        ],
        compiler_params=pltpu.CompilerParams(
            collective_id=0, has_side_effects=True, vmem_limit_bytes=48 << 20
        ),
        cost_estimate=pl.CostEstimate(
            flops=2 * slots * slots * width, bytes_accessed=4 * rows * width, transcendentals=rows
        ),
        name="nearest",
    )(embeddings, cluster_of.reshape(1, rows))
    return best.reshape(rows)


def solution(mesh):
    return jax.shard_map(
        body,
        mesh=mesh,
        in_specs=(P(("grp", "mem"), None), P(("grp", "mem"))),
        out_specs=P(("grp", "mem")),
        check_vma=False,
    )
```

time: 185 us -> 86.9 us (0.47)
  Pallas kernels: 0 us -> 83.3 us
  blocking collectives: 83.2 us -> 0 us
  matrix products: 26.4 us -> 0 us
  local copies, waits for them, and re-layouts: 22 us -> 3.47 us
  other arithmetic: 16.1 us -> 0 us
  between operations: 13.5 us -> 0.01 us
  starting transfers between devices: 12.5 us -> 0 us
  waiting for transfers between devices: 10.5 us -> 0 us
    pallas_call x0 -> x1, Pallas kernels: none -> 83.3 us  [body(): pl.pallas_call(kernel, out_shape=jax.ShapeDtypeStruct((1, rows), jnp.floa...]
    all_to_all x2 -> x0, blocking collectives: 75.3 us -> none  [the longest x1 62.4 us: body(): lax.all_to_all(send_rows, 'grp', split_axis=0, concat_axis=0, tiled=True)]
    dot_general x1 -> x0, matrix products: 26.4 us -> none  [mask_scores(): jnp.einsum('id,jd->ij', left_rows, right_rows, preferred_element_type=jnp...]
    all_to_all x2 -> x0, starting transfers between devices: 12.5 us -> none  [the longest x1 6.38 us: body(): lax.all_to_all(send_ids, 'grp', split_axis=0, concat_axis=0, tiled=True)]
    gather x1 -> x0, local copies, waits for them, and re-layouts: 10.5 us -> none  [body(): return returned[slot_index]]
    all_to_all x2 -> x0, waiting for transfers between devices: 10.5 us -> none  [the longest x1 7.08 us: body(): lax.all_to_all(send_ids, 'grp', split_axis=0, concat_axis=0, tiled=True)]
    scatter x1 -> x0, other arithmetic: 9.22 us -> none  [body(): jnp.zeros((slot_total, feature_count), jnp.bfloat16).at[slot_index]]
    scatter x2 -> x0, local copies, waits for them, and re-layouts: 8.63 us -> none  [the longest x1 4.32 us: body(): jnp.full((slot_total,), -1, jnp.int32).at[slot_index].set(anchor)]
  transfers between devices with their start and end apart: 3 -> 0, of which waited for: 2 -> 0; matrix products, arithmetic and copies ran while one was open for 6% -> 0% of each run, Pallas kernels for 0% -> 0%
where the time goes in v1:
time: 86.9 us; the launch traced here: 86.7 us
  Pallas kernels  83.3 us (96%)
  local copies, waits for them, and re-layouts  3.47 us (4%)
    pallas_call x1, Pallas kernels, body(): pl.pallas_call(kernel, out_shape=jax.ShapeDtypeStruct((1, rows), jnp.floa...  83.3 us
    unnamed x5, local copies, waits for them, and re-layouts  3.47 us

profile of v1, /device:TPU:1, one launch (start us, length us, event | category | flops | bytes accessed | tf_op | source)
XLA Modules:
  0.0 86.7 jit_solution(11828420422510506904)
XLA Ops:
  0.0 0.0 copy-start
  0.0 2.2 %copy-done = f32[1024,1024]{1,0:T(8,128)S(1)} copy-done((f32[1024,1024]{1,0:T(8,128)S(1)}, f32[1024,1024]{1,0:T(8,128)}, u32[]{:S(2)}) %copy-start) | copy-done | bytes 4194328
  2.2 0.0 copy-start.1
  2.2 0.7 copy-done.1
  2.9 83.3 %nearest.1 = f32[1,1024]{1,0:T(1,128)S(1)} custom-call(f32[1024,1024]{1,0:T(8,128)S(1)} %copy-done, s32[1,1024]{1,0:T(1,128)S(1)} %bitcast.3), custom_call_target="tpu_custom_call" | custom-call | flops 8589934592 | bytes 4194304 | tf_op jit(solution)/shard_map/nearest/pallas_call | solution.py:221
  86.1 0.6 copy.4
Async XLA Ops:
  0.0 2.2 %copy-start = (f32[1024,1024]{1,0:T(8,128)S(1)}, f32[1024,1024]{1,0:T(8,128)}, u32[]{:S(2)}) copy-start(f32[1024,1024]{1,0:T(8,128)} %emb.1) | copy-start | bytes 12582916
  2.2 0.7 copy-start.1

commit v2 on v1

--- a/solution.py
+++ b/solution.py
@@ -35,23 +35,17 @@
 ):
     rows, width = raw.shape
     grp, core = lax.axis_index("grp"), lax.axis_index("mem")
-    z, x, y = grp // 16, (grp // 4) % 4, grp % 4
-
-    def shift(k):
-        q = (k * STEP) % DEVS
-        return q // 32, (q // 8) % 4, (q // 2) % 4, q % 2
-
-    def to(k):
-        dz, dx, dy, dc = shift(k)
-        way = 1 - 2 * core
-        g = ((z + way * dz + 4) % 4) * 16 + ((x + way * dx + 4) % 4) * 4 + (y + way * dy + 4) % 4
-        return g, (core + dc) % 2
-
-    def origin(k):
-        dz, dx, dy, dc = shift(k)
-        there = (core + dc) % 2
-        way = 1 - 2 * there
-        g = ((z - way * dz + 4) % 4) * 16 + ((x - way * dx + 4) % 4) * 4 + (y - way * dy + 4) % 4
+    z, x, y = grp >> 4, (grp >> 2) & 3, grp & 3
+
+    def coords(k, away):
+        q = (k * STEP) & (DEVS - 1)
+        there = core ^ (q & 1)
+        way = 1 - 2 * core if away else 2 * there - 1
+        g = (
+            ((z + way * (q >> 5)) & 3) * 16
+            + ((x + way * ((q >> 3) & 3)) & 3) * 4
+            + ((y + way * ((q >> 1) & 3)) & 3)
+        )
         return g, there
 
     part = rows // 8
@@ -66,8 +60,11 @@
 
     barrier = pltpu.get_barrier_semaphore()
 
+    me = grp * 2 + core
+
     def greet(k, c):
-        pl.semaphore_signal(barrier, inc=1, device_id=to(k), device_id_type=MESH)
+        other = (me + k) & (DEVS - 1)
+        pl.semaphore_signal(barrier, inc=1, device_id=(other >> 1, other & 1), device_id_type=MESH)
         return c
 
     lax.fori_loop(1, DEVS, greet, 0)
@@ -109,25 +106,25 @@
         at = pl.ds(pl.multiple_of(k * SLOT, SLOT), SLOT)
         return pltpu.make_async_remote_copy(
             src_ref=send.at[at], dst_ref=recv.at[at], send_sem=send_sem, recv_sem=recv_sem.at[t],
-            device_id=to(k), device_id_type=MESH,
+            device_id=coords(k, True), device_id_type=MESH,
         )
 
     def tag_copy(k):
         return pltpu.make_async_remote_copy(
             src_ref=tag_out.at[k], dst_ref=tag_in.at[k], send_sem=tag_sems.at[0], recv_sem=tag_sems.at[1],
-            device_id=to(k), device_id_type=MESH,
+            device_id=coords(k, True), device_id_type=MESH,
         )
 
     def best_copy(k):
         return pltpu.make_async_remote_copy(
             src_ref=best_out.at[k], dst_ref=best_in.at[k], send_sem=best_sems.at[0], recv_sem=best_sems.at[1],
-            device_id=origin(k), device_id_type=MESH,
+            device_id=coords(k, False), device_id_type=MESH,
         )
 
     def whole(src, dst, sems, lo, n):
         return pltpu.make_async_remote_copy(
             src_ref=src.at[pl.ds(lo, n)], dst_ref=dst.at[pl.ds(lo, n)], send_sem=sems[0], recv_sem=sems[1],
-            device_id=to(1), device_id_type=MESH,
+            device_id=coords(1, True), device_id_type=MESH,
         )
 
     for t in range(CHUNKS):
@@ -243,7 +240,7 @@
             pltpu.SemaphoreType.DMA((2,)),
         ],
         compiler_params=pltpu.CompilerParams(
-            collective_id=0, has_side_effects=True, vmem_limit_bytes=48 << 20
+            collective_id=0, has_side_effects=True, vmem_limit_bytes=60 << 20
         ),
         cost_estimate=pl.CostEstimate(
             flops=2 * slots * slots * width, bytes_accessed=4 * rows * width, transcendentals=rows

time: 86.9 us -> 76.6 us (0.88)
  Pallas kernels: 83.3 us -> 75.2 us
  local copies, waits for them, and re-layouts: 3.47 us -> 1.28 us
    pallas_call x1, Pallas kernels: 83.3 us -> 75.2 us  [body(): pl.pallas_call(kernel, out_shape=jax.ShapeDtypeStruct((1, rows), jnp.floa...]
    unnamed x5 -> x1, local copies, waits for them, and re-layouts: 3.47 us -> 1.28 us
where the time goes in v2:
time: 76.6 us; the launch traced here: 76.5 us
  Pallas kernels  75.2 us (98%)
  local copies, waits for them, and re-layouts  1.28 us (2%)
    pallas_call x1, Pallas kernels, body(): pl.pallas_call(kernel, out_shape=jax.ShapeDtypeStruct((1, rows), jnp.floa...  75.2 us

profile of v2, /device:TPU:1, one launch (start us, length us, event | category | flops | bytes accessed | tf_op | source)
XLA Modules:
  0.0 76.5 jit_solution(13972588767153661665)
XLA Ops:
  0.0 75.2 %nearest.1 = f32[1,1024]{1,0:T(1,128)} custom-call(f32[1024,1024]{1,0:T(8,128)} %emb.1, s32[1,1024]{1,0:T(1,128)} %bitcast.3), custom_call_target="tpu_custom_call" | custom-call | flops 8589934592 | bytes 4194304 | tf_op jit(solution)/shard_map/nearest/pallas_call | solution.py:218
  75.2 1.3 %copy.4 = f32[1024]{0:T(1024)} copy(f32[1024]{0:T(1024)} %bitcast.2) | data formatting | bytes 8192

commit v3 on v2

--- a/solution.py
+++ b/solution.py
@@ -28,25 +28,33 @@
 
 
 def kernel(
-    emb, ids, out,
+    emb, ids_in, out,
     raw, normed, send, recv, tag_out, tag_in, best_out, best_in,
-    tag_col, tag_row, row_max, col_max,
+    tag_col, tag_row, row_max, col_max, ids,
     load_sem, send_sem, recv_sem, tag_sems, best_sems,
 ):
     rows, width = raw.shape
     grp, core = lax.axis_index("grp"), lax.axis_index("mem")
     z, x, y = grp >> 4, (grp >> 2) & 3, grp & 3
 
-    def coords(k, away):
+    def lines(way):
+        return [
+            [((base + way * d) & 3) * scale for d in range(4)]
+            for base, scale in ((z, 16), (x, 4), (y, 1))
+        ]
+
+    aways = lines(1 - 2 * core)
+    homes = [lines(2 * core - 1), aways]
+
+    def away(k):
         q = (k * STEP) & (DEVS - 1)
-        there = core ^ (q & 1)
-        way = 1 - 2 * core if away else 2 * there - 1
-        g = (
-            ((z + way * (q >> 5)) & 3) * 16
-            + ((x + way * ((q >> 3) & 3)) & 3) * 4
-            + ((y + way * ((q >> 1) & 3)) & 3)
-        )
-        return g, there
+        zs, xs, ys = aways
+        return zs[q >> 5] + xs[(q >> 3) & 3] + ys[(q >> 1) & 3], core ^ (q & 1)
+
+    def home(k):
+        q = (k * STEP) & (DEVS - 1)
+        zs, xs, ys = homes[q & 1]
+        return zs[q >> 5] + xs[(q >> 3) & 3] + ys[(q >> 1) & 3], core ^ (q & 1)
 
     part = rows // 8
     loads = [
@@ -55,6 +63,8 @@
         )
         for i in range(8)
     ]
+    ids_load = pltpu.make_async_copy(ids_in, ids, load_sem.at[8])
+    ids_load.start()
     for load in loads:
         load.start()
 
@@ -62,13 +72,16 @@
 
     me = grp * 2 + core
 
-    def greet(k, c):
-        other = (me + k) & (DEVS - 1)
-        pl.semaphore_signal(barrier, inc=1, device_id=(other >> 1, other & 1), device_id_type=MESH)
-        return c
-
-    lax.fori_loop(1, DEVS, greet, 0)
-
+    def greet(lo, hi):
+        for k in range(lo, hi):
+            other = (me + k) & (DEVS - 1)
+            pl.semaphore_signal(
+                barrier, inc=1, device_id=(other >> 1, other & 1), device_id_type=MESH
+            )
+
+    greet(1, DEVS)
+
+    ids_load.wait()
     cluster = ids[...]
     o_grp, o_mem, layer = cluster & 63, (cluster >> 6) & 1, cluster >> 7
     way = 1 - 2 * core
@@ -103,28 +116,28 @@
         normed[i * part : (i + 1) * part, :] = (block * factor).astype(jnp.bfloat16)
 
     def row_copy(k, t):
-        at = pl.ds(pl.multiple_of(k * SLOT, SLOT), SLOT)
+        at = pl.ds(k * SLOT, SLOT)
         return pltpu.make_async_remote_copy(
             src_ref=send.at[at], dst_ref=recv.at[at], send_sem=send_sem, recv_sem=recv_sem.at[t],
-            device_id=coords(k, True), device_id_type=MESH,
+            device_id=away(k), device_id_type=MESH,
         )
 
     def tag_copy(k):
         return pltpu.make_async_remote_copy(
             src_ref=tag_out.at[k], dst_ref=tag_in.at[k], send_sem=tag_sems.at[0], recv_sem=tag_sems.at[1],
-            device_id=coords(k, True), device_id_type=MESH,
+            device_id=away(k), device_id_type=MESH,
         )
 
     def best_copy(k):
         return pltpu.make_async_remote_copy(
             src_ref=best_out.at[k], dst_ref=best_in.at[k], send_sem=best_sems.at[0], recv_sem=best_sems.at[1],
-            device_id=coords(k, False), device_id_type=MESH,
+            device_id=home(k), device_id_type=MESH,
         )
 
     def whole(src, dst, sems, lo, n):
         return pltpu.make_async_remote_copy(
             src_ref=src.at[pl.ds(lo, n)], dst_ref=dst.at[pl.ds(lo, n)], send_sem=sems[0], recv_sem=sems[1],
-            device_id=coords(1, True), device_id_type=MESH,
+            device_id=away(1), device_id_type=MESH,
         )
 
     for t in range(CHUNKS):
@@ -134,18 +147,11 @@
             recv[:SLOT, :] = send[:SLOT, :]
             pl.semaphore_wait(barrier, DEVS - 1)
 
-        def start(k, c):
+        for k in range(max(1, t * GROUP), (t + 1) * GROUP):
             row_copy(k, t).start()
-            return c
-
-        lax.fori_loop(max(1, t * GROUP), (t + 1) * GROUP, start, 0)
         if t == 0:
-
-            def start_tag(k, c):
+            for k in range(1, DEVS):
                 tag_copy(k).start()
-                return c
-
-            lax.fori_loop(1, DEVS, start_tag, 0)
 
     whole(tag_out, tag_in, (tag_sems.at[0], tag_sems.at[1]), 1, DEVS - 1).wait()
     own_lane = iota((CHUNK, DEVS), 1) == iota((CHUNK, DEVS), 0) % SLOT
@@ -155,32 +161,32 @@
         tag_col[t * CHUNK : (t + 1) * CHUNK, :] = dot(tag, jnp.ones((DEVS, DEVS), jnp.bfloat16))
         along = dot(jnp.ones((8, DEVS), jnp.bfloat16), tag, NT)
         tag_row[:, t * CHUNK : (t + 1) * CHUNK] = jnp.where(along == 0.0, -1.0, along)
-    col_max[...] = jnp.full(col_max.shape, -1.0, jnp.float32)
-
-    def tile(t, j, diagonal, best):
-        at_t = pl.ds(pl.multiple_of(t * CHUNK, CHUNK), CHUNK)
-        at_j = pl.ds(pl.multiple_of(j * CHUNK, CHUNK), CHUNK)
-        scores = dot(recv[at_t, :], recv[at_j, :], NT)
-        col_tag = tag_col[at_t, :]
-        row_tag = tag_row[0:1, at_j]
-        allowed = jnp.concatenate([col_tag, col_tag], axis=1) == row_tag
+
+    row_max[...] = jnp.full(row_max.shape, -1.0, jnp.float32)
+
+    def meet(t, lo, n, diagonal):
+        own = recv[t * CHUNK : (t + 1) * CHUNK, :]
+        scores = dot(recv[lo : lo + n, :], own, NT)
+        tags = tag_col[lo : lo + n, :]
+        allowed = jnp.concatenate([tags, tags], axis=1) == tag_row[0:1, t * CHUNK : (t + 1) * CHUNK]
         if diagonal:
-            allowed = allowed & (iota((CHUNK, CHUNK), 0) != iota((CHUNK, CHUNK), 1))
+            allowed = allowed & (iota((n, CHUNK), 0) != iota((n, CHUNK), 1))
         scores = jnp.where(allowed, scores, -1.0)
-        if not diagonal:
-            col_max[:, at_j] = jnp.maximum(
-                col_max[:, at_j], jnp.max(scores.reshape(CHUNK // 8, 8, CHUNK), axis=0)
-            )
-        return jnp.maximum(best, jnp.maximum(scores[:, :128], scores[:, 128:]))
+        row_max[lo : lo + n, :] = jnp.maximum(
+            row_max[lo : lo + n, :], jnp.maximum(scores[:, :128], scores[:, 128:])
+        )
+        if diagonal:
+            return jnp.full((8, CHUNK), -1.0, jnp.float32)
+        return jnp.max(scores.reshape(n // 8, 8, CHUNK), axis=0)
 
     for t in range(CHUNKS):
         lo = 1 if t == 0 else t * GROUP
         n = (t + 1) * GROUP - lo
         whole(send, recv, (send_sem, recv_sem.at[t]), lo * SLOT, n * SLOT).wait_recv()
-        best = tile(t, t, True, jnp.full((CHUNK, 128), -1.0, jnp.float32))
-        if t:
-            best = lax.fori_loop(0, t, lambda j, b: tile(t, j, False, b), best)
-        row_max[t * CHUNK : (t + 1) * CHUNK, :] = best
+        best = meet(t, t * CHUNK, CHUNK, True)
+        for at in range(0, t * CHUNK, 512):
+            best = jnp.maximum(best, meet(t, at, min(512, t * CHUNK - at), False))
+        col_max[:, t * CHUNK : (t + 1) * CHUNK] = best
 
     eye = iota((128, 128), 0) == iota((128, 128), 1)
     for t in range(CHUNKS):
@@ -192,11 +198,8 @@
         laid = jnp.where(own_lane, best, -1.0).reshape(GROUP, SLOT, DEVS)
         best_out[t * GROUP : (t + 1) * GROUP] = jnp.max(laid, axis=1, keepdims=True)
 
-        def give(k, c):
+        for k in range(max(1, t * GROUP), (t + 1) * GROUP):
             best_copy(k).start()
-            return c
-
-        lax.fori_loop(max(1, t * GROUP), (t + 1) * GROUP, give, 0)
         if t == 0:
             best_in[0] = best_out[0]
 
@@ -218,7 +221,7 @@
     best = pl.pallas_call(
         kernel,
         out_shape=jax.ShapeDtypeStruct((1, rows), jnp.float32),
-        in_specs=[pl.BlockSpec(memory_space=pl.ANY), pl.BlockSpec(memory_space=pltpu.VMEM)],
+        in_specs=[pl.BlockSpec(memory_space=pl.ANY), pl.BlockSpec(memory_space=pl.ANY)],
         out_specs=pl.BlockSpec(memory_space=pltpu.VMEM),
         scratch_shapes=[
             pltpu.VMEM((rows, width), jnp.float32),
@@ -233,7 +236,8 @@
             pltpu.VMEM((8, slots), jnp.float32),
             pltpu.VMEM((slots, 128), jnp.float32),
             pltpu.VMEM((8, slots), jnp.float32),
-            pltpu.SemaphoreType.DMA((8,)),
+            pltpu.VMEM((1, rows), jnp.int32),
+            pltpu.SemaphoreType.DMA((9,)),
             pltpu.SemaphoreType.DMA,
             pltpu.SemaphoreType.DMA((CHUNKS,)),
             pltpu.SemaphoreType.DMA((2,)),

time: 76.6 us -> 70.3 us (0.918)
  Pallas kernels: 75.2 us -> 68.9 us
    pallas_call x1, Pallas kernels: 75.2 us -> 68.9 us  [body(): pl.pallas_call(kernel, out_shape=jax.ShapeDtypeStruct((1, rows), jnp.floa...]
where the time goes in v3:
time: 70.3 us; the launch traced here: 70.2 us
  Pallas kernels  68.9 us (98%)
  local copies, waits for them, and re-layouts  1.28 us (2%)
    pallas_call x1, Pallas kernels, body(): pl.pallas_call(kernel, out_shape=jax.ShapeDtypeStruct((1, rows), jnp.floa...  68.9 us

profile of v3, /device:TPU:1, one launch (start us, length us, event | category | flops | bytes accessed | tf_op | source)
XLA Modules:
  0.0 70.2 jit_solution(4998994562636690560)
XLA Ops:
  0.0 68.9 %nearest.1 = f32[1,1024]{1,0:T(1,128)} custom-call(f32[1024,1024]{1,0:T(8,128)} %emb.1, s32[1,1024]{1,0:T(1,128)} %bitcast.3), custom_call_target="tpu_custom_call" | custom-call | flops 8589934592 | bytes 4194304 | tf_op jit(solution)/shard_map/nearest/pallas_call | solution.py:221
  68.9 1.3 %copy.4 = f32[1024]{0:T(1024)} copy(f32[1024]{0:T(1024)} %bitcast.2) | data formatting | bytes 8192

commit v4 on v3

--- a/solution.py
+++ b/solution.py
@@ -9,9 +9,28 @@
 from jax.sharding import PartitionSpec as P
 
 MESH = pl.DeviceIdType.MESH
-STEP = 115
-BACK = 59
 DEVS = 128
+
+
+def axes(q):
+    return (q >> 5 != 0) + ((q >> 3) & 3 != 0) + ((q >> 1) & 3 != 0)
+
+
+LCG = [(115 * k) % DEVS for k in range(DEVS)]
+def spread(a, b):
+    n = len(a) + len(b)
+    out, i = [], 0
+    for k in range(n):
+        if (k + 1) * len(a) // n > i:
+            out.append(a[i])
+            i += 1
+        else:
+            out.append(b[k - i])
+    return out
+
+
+ONE, TWO, THREE = ([q for q in LCG if q and max(1, axes(q)) == n] for n in (1, 2, 3))
+ORDER = [0] + ONE + TWO[:24] + spread(TWO[24:], THREE)
 SLOT = 16
 GROUP = 16
 CHUNK = GROUP * SLOT
@@ -28,10 +47,10 @@
 
 
 def kernel(
-    emb, ids_in, out,
+    emb, ids_in, order_in, order_row_in, out,
     raw, normed, send, recv, tag_out, tag_in, best_out, best_in,
-    tag_col, tag_row, row_max, col_max, ids,
-    load_sem, send_sem, recv_sem, tag_sems, best_sems,
+    tag_col, tag_row, row_max, col_max, ids, order, order_row, laid,
+    load_sem, send_sem, recv_sem, tag_sems, best_sems, entry_sems,
 ):
     rows, width = raw.shape
     grp, core = lax.axis_index("grp"), lax.axis_index("mem")
@@ -44,16 +63,12 @@
         ]
 
     aways = lines(1 - 2 * core)
-    homes = [lines(2 * core - 1), aways]
+    aways = lines(1 - 2 * core)
+    me = grp * 2 + core
 
     def away(k):
-        q = (k * STEP) & (DEVS - 1)
+        q = ORDER[k]
         zs, xs, ys = aways
-        return zs[q >> 5] + xs[(q >> 3) & 3] + ys[(q >> 1) & 3], core ^ (q & 1)
-
-    def home(k):
-        q = (k * STEP) & (DEVS - 1)
-        zs, xs, ys = homes[q & 1]
         return zs[q >> 5] + xs[(q >> 3) & 3] + ys[(q >> 1) & 3], core ^ (q & 1)
 
     part = rows // 8
@@ -65,21 +80,38 @@
     ]
     ids_load = pltpu.make_async_copy(ids_in, ids, load_sem.at[8])
     ids_load.start()
+    order_load = pltpu.make_async_copy(order_in, order, load_sem.at[9])
+    order_load.start()
+    row_load = pltpu.make_async_copy(order_row_in, order_row, load_sem.at[10])
+    row_load.start()
     for load in loads:
         load.start()
 
     barrier = pltpu.get_barrier_semaphore()
 
-    me = grp * 2 + core
-
-    def greet(lo, hi):
-        for k in range(lo, hi):
-            other = (me + k) & (DEVS - 1)
-            pl.semaphore_signal(
-                barrier, inc=1, device_id=(other >> 1, other & 1), device_id_type=MESH
-            )
-
-    greet(1, DEVS)
+    def greet(sem, other):
+        pl.semaphore_signal(sem, inc=1, device_id=other, device_id_type=MESH)
+
+    zs, xs, ys = aways
+    z_line = [zs[d] + xs[0] + ys[0] for d in range(1, 4)]
+    x_line = [zs[0] + xs[d] + ys[0] for d in range(1, 4)]
+    y_line = [zs[0] + xs[0] + ys[d] for d in range(1, 4)]
+    greet(barrier, (grp, core ^ 1))
+    for chip in z_line + x_line + y_line:
+        greet(barrier, (chip, core))
+        greet(barrier, (chip, core ^ 1))
+
+    def enter(stage):
+        if stage == 1:
+            pl.semaphore_wait(barrier, 19)
+            for chip in z_line + x_line + y_line:
+                greet(entry_sems.at[0], (chip, core))
+        elif stage == 2:
+            pl.semaphore_wait(entry_sems.at[0], 9)
+            for chip in z_line:
+                greet(entry_sems.at[1], (chip, core))
+        else:
+            pl.semaphore_wait(entry_sems.at[1], 3)
 
     ids_load.wait()
     cluster = ids[...]
@@ -89,19 +121,30 @@
     dx = (way * (((o_grp >> 2) & 3) - x)) & 3
     dy = (way * ((o_grp & 3) - y)) & 3
     dc = (o_mem - core) & 1
-    place = ((dz * 32 + dx * 8 + dy * 2 + dc) * BACK) & (DEVS - 1)
-    owner_is = (iota((DEVS, rows), 0) == place).astype(jnp.float32)
+    order_load.wait()
+    row_load.wait()
+    shift = order_row[...]
+    there = core ^ (shift & 1)
+    back = 2 * there - 1
+    source = (
+        ((z + back * (shift >> 5)) & 3) * 32
+        + ((x + back * ((shift >> 3) & 3)) & 3) * 8
+        + ((y + back * ((shift >> 1) & 3)) & 3) * 2
+        + there
+    )
+    to_source = (iota((DEVS, DEVS), 0) == source).astype(jnp.float32).astype(jnp.bfloat16)
+    owner_is = (order[...] == dz * 32 + dx * 8 + dy * 2 + dc).astype(jnp.float32)
     owner_bf = owner_is.astype(jnp.bfloat16)
     upper = (iota((256, 256), 0) < iota((256, 256), 1)).astype(jnp.bfloat16)
-    before = jnp.zeros((DEVS, 1), jnp.float32)
-    ranks = []
+    before = (iota((DEVS, 1), 0) * SLOT).astype(jnp.float32)
+    slots = []
     for i in range(rows // 256):
         block = owner_is[:, i * 256 : (i + 1) * 256]
         ahead = dot(owner_bf[:, i * 256 : (i + 1) * 256], upper) + before
-        ranks.append(jnp.sum(block * ahead, axis=0, keepdims=True))
+        slots.append(jnp.sum(block * ahead, axis=0, keepdims=True))
         before = before + jnp.sum(block, axis=1, keepdims=True)
-    rank = jnp.concatenate(ranks, axis=1).astype(jnp.int32)
-    slot = place * SLOT + rank
+    slot = jnp.concatenate(slots, axis=1).astype(jnp.int32)
+    rank = slot & (SLOT - 1)
     rank_is = iota((DEVS, rows), 0) == rank
     tags = dot(
         owner_bf, jnp.where(rank_is, (layer + 1).astype(jnp.float32), 0.0).astype(jnp.bfloat16), NT
@@ -124,14 +167,16 @@
 
     def tag_copy(k):
         return pltpu.make_async_remote_copy(
-            src_ref=tag_out.at[k], dst_ref=tag_in.at[k], send_sem=tag_sems.at[0], recv_sem=tag_sems.at[1],
+            src_ref=tag_out.at[k], dst_ref=tag_in.at[k], send_sem=tag_sems.at[0], recv_sem=tag_sems.at[1 + k // GROUP],
             device_id=away(k), device_id_type=MESH,
         )
 
-    def best_copy(k):
+    def best_copy(plane, dx, dy, dc):
+        chip, there = plane * 16 + xs[dx] + ys[dy], core ^ dc
         return pltpu.make_async_remote_copy(
-            src_ref=best_out.at[k], dst_ref=best_in.at[k], send_sem=best_sems.at[0], recv_sem=best_sems.at[1],
-            device_id=home(k), device_id_type=MESH,
+            src_ref=best_out.at[chip * 2 + there], dst_ref=best_in.at[me],
+            send_sem=best_sems.at[0], recv_sem=best_sems.at[1],
+            device_id=(chip, there), device_id_type=MESH,
         )
 
     def whole(src, dst, sems, lo, n):
@@ -140,28 +185,21 @@
             device_id=away(1), device_id_type=MESH,
         )
 
+    stage = 0
     for t in range(CHUNKS):
         pick = (iota((CHUNK, rows), 0) + t * CHUNK == slot).astype(jnp.float32).astype(jnp.bfloat16)
         send[t * CHUNK : (t + 1) * CHUNK, :] = dot(pick, normed[...]).astype(jnp.bfloat16)
         if t == 0:
             recv[:SLOT, :] = send[:SLOT, :]
-            pl.semaphore_wait(barrier, DEVS - 1)
-
         for k in range(max(1, t * GROUP), (t + 1) * GROUP):
+            need = max(1, axes(ORDER[k]))
+            while stage < need:
+                stage += 1
+                enter(stage)
+            tag_copy(k).start()
             row_copy(k, t).start()
-        if t == 0:
-            for k in range(1, DEVS):
-                tag_copy(k).start()
-
-    whole(tag_out, tag_in, (tag_sems.at[0], tag_sems.at[1]), 1, DEVS - 1).wait()
+
     own_lane = iota((CHUNK, DEVS), 1) == iota((CHUNK, DEVS), 0) % SLOT
-    for t in range(CHUNKS):
-        spread = jnp.broadcast_to(tag_in[t * GROUP : (t + 1) * GROUP], (GROUP, SLOT, DEVS))
-        tag = jnp.where(own_lane, spread.reshape(CHUNK, DEVS), 0.0).astype(jnp.bfloat16)
-        tag_col[t * CHUNK : (t + 1) * CHUNK, :] = dot(tag, jnp.ones((DEVS, DEVS), jnp.bfloat16))
-        along = dot(jnp.ones((8, DEVS), jnp.bfloat16), tag, NT)
-        tag_row[:, t * CHUNK : (t + 1) * CHUNK] = jnp.where(along == 0.0, -1.0, along)
-
     row_max[...] = jnp.full(row_max.shape, -1.0, jnp.float32)
 
     def meet(t, lo, n, diagonal):
@@ -183,6 +221,12 @@
         lo = 1 if t == 0 else t * GROUP
         n = (t + 1) * GROUP - lo
         whole(send, recv, (send_sem, recv_sem.at[t]), lo * SLOT, n * SLOT).wait_recv()
+        whole(tag_out, tag_in, (tag_sems.at[0], tag_sems.at[1 + t]), lo, n).wait_recv()
+        spread_tag = jnp.broadcast_to(tag_in[t * GROUP : (t + 1) * GROUP], (GROUP, SLOT, DEVS))
+        tag = jnp.where(own_lane, spread_tag.reshape(CHUNK, DEVS), 0.0).astype(jnp.bfloat16)
+        tag_col[t * CHUNK : (t + 1) * CHUNK, :] = dot(tag, jnp.ones((DEVS, DEVS), jnp.bfloat16))
+        along = dot(jnp.ones((8, DEVS), jnp.bfloat16), tag, NT)
+        tag_row[:, t * CHUNK : (t + 1) * CHUNK] = jnp.where(along == 0.0, -1.0, along)
         best = meet(t, t * CHUNK, CHUNK, True)
         for at in range(0, t * CHUNK, 512):
             best = jnp.maximum(best, meet(t, at, min(512, t * CHUNK - at), False))
@@ -195,33 +239,48 @@
             [jnp.where(eye, along[:, :128], -1.0), jnp.where(eye, along[:, 128:], -1.0)], axis=0
         )
         best = jnp.max(jnp.maximum(row_max[t * CHUNK : (t + 1) * CHUNK, :], turned), axis=1, keepdims=True)
-        laid = jnp.where(own_lane, best, -1.0).reshape(GROUP, SLOT, DEVS)
-        best_out[t * GROUP : (t + 1) * GROUP] = jnp.max(laid, axis=1, keepdims=True)
-
-        for k in range(max(1, t * GROUP), (t + 1) * GROUP):
-            best_copy(k).start()
-        if t == 0:
-            best_in[0] = best_out[0]
+        blocks = jnp.where(own_lane, best, -1.0).reshape(GROUP, SLOT, DEVS)
+        laid[t * GROUP : (t + 1) * GROUP, :] = jnp.max(blocks, axis=1)
+
+    def exact(rest, pick):
+        total = None
+        for _ in range(3):
+            piece = rest.astype(jnp.bfloat16)
+            rest = rest - piece.astype(jnp.float32)
+            term = pick(piece)
+            total = term if total is None else total + term
+        return total
+
+    best_out[...] = exact(laid[...], lambda piece: dot(to_source, piece)).reshape(DEVS, 1, DEVS)
+    best_in[me] = best_out[me]
+    for plane in range(4):
+        for step in range(32):
+            if step == 0:
+
+                @pl.when(plane != z)
+                def _():
+                    best_copy(plane, 0, 0, 0).start()
+
+            else:
+                best_copy(plane, step >> 3, (step >> 1) & 3, step & 1).start()
 
     whole(send, recv, (send_sem, recv_sem.at[0]), SLOT, (DEVS - 1) * SLOT).wait_send()
+    whole(tag_out, tag_in, (tag_sems.at[0], tag_sems.at[1]), 1, DEVS - 1).wait_send()
     whole(best_out, best_in, (best_sems.at[0], best_sems.at[1]), 1, DEVS - 1).wait()
     rank_bf = rank_is.astype(jnp.float32).astype(jnp.bfloat16)
-    rest = best_in[...].reshape(DEVS, DEVS)
-    found = jnp.zeros((DEVS, rows), jnp.float32)
-    for _ in range(3):
-        piece = rest.astype(jnp.bfloat16)
-        rest = rest - piece.astype(jnp.float32)
-        found = found + dot(piece, rank_bf)
-    out[...] = jnp.sum(owner_is * found, axis=0, keepdims=True)
+    found = exact(best_in[...].reshape(DEVS, DEVS), lambda piece: dot(piece, rank_bf))
+    owner = o_grp * 2 + o_mem
+    out[...] = jnp.sum(jnp.where(iota((DEVS, rows), 0) == owner, found, 0.0), axis=0, keepdims=True)
 
 
 def body(embeddings, cluster_of):
     rows, width = embeddings.shape
     slots = DEVS * SLOT
+    order = jnp.array(ORDER, jnp.int32)
     best = pl.pallas_call(
         kernel,
         out_shape=jax.ShapeDtypeStruct((1, rows), jnp.float32),
-        in_specs=[pl.BlockSpec(memory_space=pl.ANY), pl.BlockSpec(memory_space=pl.ANY)],
+        in_specs=[pl.BlockSpec(memory_space=pl.ANY)] * 4,
         out_specs=pl.BlockSpec(memory_space=pltpu.VMEM),
         scratch_shapes=[
             pltpu.VMEM((rows, width), jnp.float32),
@@ -237,11 +296,15 @@
             pltpu.VMEM((slots, 128), jnp.float32),
             pltpu.VMEM((8, slots), jnp.float32),
             pltpu.VMEM((1, rows), jnp.int32),
-            pltpu.SemaphoreType.DMA((9,)),
+            pltpu.VMEM((DEVS, 1), jnp.int32),
+            pltpu.VMEM((1, DEVS), jnp.int32),
+            pltpu.VMEM((DEVS, DEVS), jnp.float32),
+            pltpu.SemaphoreType.DMA((11,)),
             pltpu.SemaphoreType.DMA,
             pltpu.SemaphoreType.DMA((CHUNKS,)),
+            pltpu.SemaphoreType.DMA((1 + CHUNKS,)),
             pltpu.SemaphoreType.DMA((2,)),
-            pltpu.SemaphoreType.DMA((2,)),
+            pltpu.SemaphoreType.REGULAR((2,)),
         ],
         compiler_params=pltpu.CompilerParams(
             collective_id=0, has_side_effects=True, vmem_limit_bytes=60 << 20
@@ -250,7 +313,7 @@
             flops=2 * slots * slots * width, bytes_accessed=4 * rows * width, transcendentals=rows
         ),
         name="nearest",
-    )(embeddings, cluster_of.reshape(1, rows))
+    )(embeddings, cluster_of.reshape(1, rows), order.reshape(DEVS, 1), order.reshape(1, DEVS))
     return best.reshape(rows)
 
 

time: 70.3 us -> 68.6 us (0.976)
  Pallas kernels: 68.9 us -> 67.2 us
    pallas_call x1, Pallas kernels: 68.9 us -> 67.2 us  [body(): pl.pallas_call(kernel, out_shape=jax.ShapeDtypeStruct((1, rows), jnp.floa...]
where the time goes in v4:
time: 68.6 us; the launch traced here: 68.4 us
  Pallas kernels  67.2 us (98%)
  local copies, waits for them, and re-layouts  1.28 us (2%)
    pallas_call x1, Pallas kernels, body(): pl.pallas_call(kernel, out_shape=jax.ShapeDtypeStruct((1, rows), jnp.floa...  67.2 us

profile of v4, /device:TPU:1, one launch (start us, length us, event | category | flops | bytes accessed | tf_op | source)
XLA Modules:
  0.0 68.4 jit_solution(8633220087111652238)
XLA Ops:
  0.0 67.2 %nearest.1 = f32[1,1024]{1,0:T(1,128)} custom-call(f32[1024,1024]{1,0:T(8,128)} %emb.1, s32[1,1024]{1,0:T(1,128)} %bitcast.3, s32[128,1]{1,0:T(8,128)} %constant.3.order_in, s32[1,128]{1,0:T(1,128)} %constant.4.order_row_in), custom_call_target="tpu_custom_call" | custom-call | flops 8589934592 | bytes 4194304 | tf_op jit(solution)/shard_map/nearest/pallas_call | solution.py:280
  67.2 1.3 %copy.5 = f32[1024]{0:T(1024)} copy(f32[1024]{0:T(1024)} %bitcast.2) | data formatting | bytes 8192

commit v5 on v4

--- a/solution.py
+++ b/solution.py
@@ -16,7 +16,7 @@
     return (q >> 5 != 0) + ((q >> 3) & 3 != 0) + ((q >> 1) & 3 != 0)
 
 
-LCG = [(115 * k) % DEVS for k in range(DEVS)]
+LCG = [(107 * k) % DEVS for k in range(DEVS)]
 def spread(a, b):
     n = len(a) + len(b)
     out, i = [], 0
@@ -47,9 +47,9 @@
 
 
 def kernel(
-    emb, ids_in, order_in, order_row_in, out,
+    emb, ids_in, out,
     raw, normed, send, recv, tag_out, tag_in, best_out, best_in,
-    tag_col, tag_row, row_max, col_max, ids, order, order_row, laid,
+    tag_col, tag_row, row_max, col_max, ids, laid,
     load_sem, send_sem, recv_sem, tag_sems, best_sems, entry_sems,
 ):
     rows, width = raw.shape
@@ -80,10 +80,6 @@
     ]
     ids_load = pltpu.make_async_copy(ids_in, ids, load_sem.at[8])
     ids_load.start()
-    order_load = pltpu.make_async_copy(order_in, order, load_sem.at[9])
-    order_load.start()
-    row_load = pltpu.make_async_copy(order_row_in, order_row, load_sem.at[10])
-    row_load.start()
     for load in loads:
         load.start()
 
@@ -113,6 +109,18 @@
         else:
             pl.semaphore_wait(entry_sems.at[1], 3)
 
+    lane = iota((1, DEVS), 1)
+    parts = []
+    for first in range(0, DEVS, 16):
+        part_of = jnp.zeros((1, DEVS), jnp.int32)
+        for k in range(first, first + 16):
+            part_of = jnp.where(lane == k, ORDER[k], part_of)
+        parts.append(part_of)
+    shift = functools.reduce(jnp.add, parts)
+    order = jnp.sum(
+        jnp.where(iota((DEVS, DEVS), 0) == iota((DEVS, DEVS), 1), shift, 0).astype(jnp.float32),
+        axis=1, keepdims=True,
+    ).astype(jnp.int32)
     ids_load.wait()
     cluster = ids[...]
     o_grp, o_mem, layer = cluster & 63, (cluster >> 6) & 1, cluster >> 7
@@ -121,9 +129,6 @@
     dx = (way * (((o_grp >> 2) & 3) - x)) & 3
     dy = (way * ((o_grp & 3) - y)) & 3
     dc = (o_mem - core) & 1
-    order_load.wait()
-    row_load.wait()
-    shift = order_row[...]
     there = core ^ (shift & 1)
     back = 2 * there - 1
     source = (
@@ -133,7 +138,7 @@
         + there
     )
     to_source = (iota((DEVS, DEVS), 0) == source).astype(jnp.float32).astype(jnp.bfloat16)
-    owner_is = (order[...] == dz * 32 + dx * 8 + dy * 2 + dc).astype(jnp.float32)
+    owner_is = (order == dz * 32 + dx * 8 + dy * 2 + dc).astype(jnp.float32)
     owner_bf = owner_is.astype(jnp.bfloat16)
     upper = (iota((256, 256), 0) < iota((256, 256), 1)).astype(jnp.bfloat16)
     before = (iota((DEVS, 1), 0) * SLOT).astype(jnp.float32)
@@ -276,11 +281,10 @@
 def body(embeddings, cluster_of):
     rows, width = embeddings.shape
     slots = DEVS * SLOT
-    order = jnp.array(ORDER, jnp.int32)
     best = pl.pallas_call(
         kernel,
         out_shape=jax.ShapeDtypeStruct((1, rows), jnp.float32),
-        in_specs=[pl.BlockSpec(memory_space=pl.ANY)] * 4,
+        in_specs=[pl.BlockSpec(memory_space=pl.ANY)] * 2,
         out_specs=pl.BlockSpec(memory_space=pltpu.VMEM),
         scratch_shapes=[
             pltpu.VMEM((rows, width), jnp.float32),
@@ -296,10 +300,8 @@
             pltpu.VMEM((slots, 128), jnp.float32),
             pltpu.VMEM((8, slots), jnp.float32),
             pltpu.VMEM((1, rows), jnp.int32),
-            pltpu.VMEM((DEVS, 1), jnp.int32),
-            pltpu.VMEM((1, DEVS), jnp.int32),
             pltpu.VMEM((DEVS, DEVS), jnp.float32),
-            pltpu.SemaphoreType.DMA((11,)),
+            pltpu.SemaphoreType.DMA((9,)),
             pltpu.SemaphoreType.DMA,
             pltpu.SemaphoreType.DMA((CHUNKS,)),
             pltpu.SemaphoreType.DMA((1 + CHUNKS,)),
@@ -307,13 +309,13 @@
             pltpu.SemaphoreType.REGULAR((2,)),
         ],
         compiler_params=pltpu.CompilerParams(
-            collective_id=0, has_side_effects=True, vmem_limit_bytes=60 << 20
+            collective_id=0, has_side_effects=True, vmem_limit_bytes=52 << 20
         ),
         cost_estimate=pl.CostEstimate(
             flops=2 * slots * slots * width, bytes_accessed=4 * rows * width, transcendentals=rows
         ),
         name="nearest",
-    )(embeddings, cluster_of.reshape(1, rows), order.reshape(DEVS, 1), order.reshape(1, DEVS))
+    )(embeddings, cluster_of.reshape(1, rows))
     return best.reshape(rows)
 
 

time: 68.6 us -> 67.2 us (0.980)
  Pallas kernels: 67.2 us -> 65.8 us
    pallas_call x1, Pallas kernels: 67.2 us -> 65.8 us  [body(): pl.pallas_call(kernel, out_shape=jax.ShapeDtypeStruct((1, rows), jnp.floa...]
where the time goes in v5:
time: 67.2 us; the launch traced here: 67.1 us
  Pallas kernels  65.8 us (98%)
  local copies, waits for them, and re-layouts  1.28 us (2%)
    pallas_call x1, Pallas kernels, body(): pl.pallas_call(kernel, out_shape=jax.ShapeDtypeStruct((1, rows), jnp.floa...  65.8 us

profile of v5, /device:TPU:1, one launch (start us, length us, event | category | flops | bytes accessed | tf_op | source)
XLA Modules:
  0.0 67.1 jit_solution(18135416148775102982)
XLA Ops:
  0.0 0.0 copy-start
  0.0 0.7 %copy-done = s32[1024]{0:T(1024)S(1)} copy-done((s32[1024]{0:T(1024)S(1)}, s32[1024]{0:T(1024)}, u32[]{:S(2)}) %copy-start) | copy-done | bytes 4120
  0.7 65.8 %nearest.1 = f32[1,1024]{1,0:T(1,128)S(1)} custom-call(f32[1024,1024]{1,0:T(8,128)} %emb.1, s32[1,1024]{1,0:T(1,128)S(1)} %bitcast.3), custom_call_target="tpu_custom_call" | custom-call | flops 8589934592 | bytes 4194304 | tf_op jit(solution)/shard_map/nearest/pallas_call | solution.py:284
  66.5 0.6 copy.4
Async XLA Ops:
  0.0 0.7 %copy-start = (s32[1024]{0:T(1024)S(1)}, s32[1024]{0:T(1024)}, u32[]{:S(2)}) copy-start(s32[1024]{0:T(1024)} %param.3) | copy-start | bytes 12292

commit v6 on v5

--- a/solution.py
+++ b/solution.py
@@ -154,7 +154,7 @@
     tags = dot(
         owner_bf, jnp.where(rank_is, (layer + 1).astype(jnp.float32), 0.0).astype(jnp.bfloat16), NT
     )
-    tag_out[...] = tags.reshape(DEVS, 1, DEVS)
+    tag_out[...] = tags[:, :SLOT].reshape(DEVS, 1, SLOT)
     tag_in[0] = tag_out[0]
 
     for i in range(8):
@@ -227,10 +227,10 @@
         n = (t + 1) * GROUP - lo
         whole(send, recv, (send_sem, recv_sem.at[t]), lo * SLOT, n * SLOT).wait_recv()
         whole(tag_out, tag_in, (tag_sems.at[0], tag_sems.at[1 + t]), lo, n).wait_recv()
-        spread_tag = jnp.broadcast_to(tag_in[t * GROUP : (t + 1) * GROUP], (GROUP, SLOT, DEVS))
-        tag = jnp.where(own_lane, spread_tag.reshape(CHUNK, DEVS), 0.0).astype(jnp.bfloat16)
-        tag_col[t * CHUNK : (t + 1) * CHUNK, :] = dot(tag, jnp.ones((DEVS, DEVS), jnp.bfloat16))
-        along = dot(jnp.ones((8, DEVS), jnp.bfloat16), tag, NT)
+        spread_tag = jnp.broadcast_to(tag_in[t * GROUP : (t + 1) * GROUP], (GROUP, SLOT, SLOT))
+        tag = jnp.where(own_lane[:, :SLOT], spread_tag.reshape(CHUNK, SLOT), 0.0).astype(jnp.bfloat16)
+        tag_col[t * CHUNK : (t + 1) * CHUNK, :] = dot(tag, jnp.ones((SLOT, DEVS), jnp.bfloat16))
+        along = dot(jnp.ones((8, SLOT), jnp.bfloat16), tag, NT)
         tag_row[:, t * CHUNK : (t + 1) * CHUNK] = jnp.where(along == 0.0, -1.0, along)
         best = meet(t, t * CHUNK, CHUNK, True)
         for at in range(0, t * CHUNK, 512):
@@ -256,7 +256,7 @@
             total = term if total is None else total + term
         return total
 
-    best_out[...] = exact(laid[...], lambda piece: dot(to_source, piece)).reshape(DEVS, 1, DEVS)
+    best_out[...] = exact(laid[...], lambda piece: dot(to_source, piece))[:, :SLOT].reshape(DEVS, 1, SLOT)
     best_in[me] = best_out[me]
     for plane in range(4):
         for step in range(32):
@@ -269,12 +269,14 @@
             else:
                 best_copy(plane, step >> 3, (step >> 1) & 3, step & 1).start()
 
+    returns = whole(best_out, best_in, (best_sems.at[0], best_sems.at[1]), 1, DEVS - 1)
+    returns.wait_recv()
+    rank_bf = rank_is.astype(jnp.float32).astype(jnp.bfloat16)
+    found = exact(best_in[...].reshape(DEVS, SLOT), lambda piece: dot(piece, rank_bf[:SLOT, :]))
+    owner = o_grp * 2 + o_mem
+    returns.wait_send()
     whole(send, recv, (send_sem, recv_sem.at[0]), SLOT, (DEVS - 1) * SLOT).wait_send()
     whole(tag_out, tag_in, (tag_sems.at[0], tag_sems.at[1]), 1, DEVS - 1).wait_send()
-    whole(best_out, best_in, (best_sems.at[0], best_sems.at[1]), 1, DEVS - 1).wait()
-    rank_bf = rank_is.astype(jnp.float32).astype(jnp.bfloat16)
-    found = exact(best_in[...].reshape(DEVS, DEVS), lambda piece: dot(piece, rank_bf))
-    owner = o_grp * 2 + o_mem
     out[...] = jnp.sum(jnp.where(iota((DEVS, rows), 0) == owner, found, 0.0), axis=0, keepdims=True)
 
 
@@ -291,10 +293,10 @@
             pltpu.VMEM((rows, width), jnp.bfloat16),
             pltpu.VMEM((slots, width), jnp.bfloat16),
             pltpu.VMEM((slots, width), jnp.bfloat16),
-            pltpu.VMEM((DEVS, 1, DEVS), jnp.float32),
-            pltpu.VMEM((DEVS, 1, DEVS), jnp.float32),
-            pltpu.VMEM((DEVS, 1, DEVS), jnp.float32),
-            pltpu.VMEM((DEVS, 1, DEVS), jnp.float32),
+            pltpu.VMEM((DEVS, 1, SLOT), jnp.float32),
+            pltpu.VMEM((DEVS, 1, SLOT), jnp.float32),
+            pltpu.VMEM((DEVS, 1, SLOT), jnp.float32),
+            pltpu.VMEM((DEVS, 1, SLOT), jnp.float32),
             pltpu.VMEM((slots, 128), jnp.float32),
             pltpu.VMEM((8, slots), jnp.float32),
             pltpu.VMEM((slots, 128), jnp.float32),

time: 67.2 us -> 67.4 us (level)
  no operation moved by 1% of the time
where the time goes in v6:
time: 67.4 us; the launch traced here: 67.2 us
  Pallas kernels  65.9 us (98%)
  local copies, waits for them, and re-layouts  1.28 us (2%)
    pallas_call x1, Pallas kernels, body(): pl.pallas_call(kernel, out_shape=jax.ShapeDtypeStruct((1, rows), jnp.floa...  65.9 us

profile of v6, /device:TPU:1, one launch (start us, length us, event | category | flops | bytes accessed | tf_op | source)
XLA Modules:
  0.0 67.2 jit_solution(14515563827170428808)
XLA Ops:
  0.0 0.0 copy-start
  0.0 0.7 %copy-done = s32[1024]{0:T(1024)S(1)} copy-done((s32[1024]{0:T(1024)S(1)}, s32[1024]{0:T(1024)}, u32[]{:S(2)}) %copy-start) | copy-done | bytes 4120
  0.7 65.9 %nearest.1 = f32[1,1024]{1,0:T(1,128)S(1)} custom-call(f32[1024,1024]{1,0:T(8,128)} %emb.1, s32[1,1024]{1,0:T(1,128)S(1)} %bitcast.3), custom_call_target="tpu_custom_call" | custom-call | flops 8589934592 | bytes 4194304 | tf_op jit(solution)/shard_map/nearest/pallas_call | solution.py:286
  66.6 0.6 copy.4
Async XLA Ops:
  0.0 0.7 %copy-start = (s32[1024]{0:T(1024)S(1)}, s32[1024]{0:T(1024)}, u32[]{:S(2)}) copy-start(s32[1024]{0:T(1024)} %param.3) | copy-start | bytes 12292
